TPU v7x, 256 devices: a whole 4x4x8 slice. The times are simulated.
256 devices in a mesh: prow: 32 (over x, z), pcol: 8 (over y, core).
Axes of the slice: x: 4, y: 4, z: 8, core: 2. Of those that a mesh axis runs over, the one named last changes fastest.
Arguments:
- matrix: bfloat16 [32, 3, 256, 8, 12, 256], P('prow', None, None, 'pcol')
- row_perm: int32 [32, 3, 256], P('prow'), may hold values from 0 to 255, as said below
- block_pattern: int32 [96, 96], replicated, may hold values from 0 to 1, as said below
Outputs:
- factored: bfloat16 [32, 3, 256, 8, 12, 256], P('prow', None, None, 'pcol')
Inputs may be any that keep to these rules, and one draw needn't show every extreme that they name: `row_perm`: each row of 256 entries along the last dimension is a permutation of 0 to 255. `block_pattern`: 0 or 1. Diagonal blocks are 1 and block (1, 0) is 0. The pattern is closed under the fill of supernodes 0 and 1: if (i, k) and (k, j) are 1 with i > k and j > k, then (i, j) is 1 (for k = 1 after the fill of k = 0). For k = 0 and k = 1, the blocks (k, j) with j >= k that lie in one process-grid column (j % 8 fixed) hold at most 6 ones, and exactly 6 in some process-grid column.
All inputs are finite; a program needn't handle non-finite values.
Results may differ from a plain program's by a relative error of at most 0.0028.
Values may be sent and summed in bfloat16 or wider, within the bound.
No kernel may reach another device: no remote copies, remote signals or barrier semaphores. Data moves between devices by JAX's collectives and lax.ppermute only.
A program may use at most 128 MiB of HBM per device.

v0:
```python
import functools

import jax
import jax.numpy as jnp
from jax import lax
from jax.experimental import pallas as pl
from jax.experimental.pallas import tpu as pltpu
from jax.sharding import PartitionSpec as P

B = 256
LR = 3
LC = 12
NB = 96
UCAP = 6
NEWTON = 3
ROWS_GRID = 32
COLS_GRID = 8
NX = 4
NZ = 8
PIECE = B // NX
SELECT_BYTES = 8 << 20
MIB = 1 << 20

F32 = jnp.float32
BF16 = jnp.bfloat16

FAR_UP = ([(0, 3)], [(1, 4)])
FAR_DOWN = ([(0, 5)], [(1, 6)])
NEAR_UP = ([(0, 1), (3, 4), (5, 6)], [(1, 2), (4, 5), (6, 7)])
NEAR_DOWN = ([(0, 7), (3, 2)], [(1, 0), (4, 3)])
FROM_0 = "hudhuhud"
FROM_1 = "dhudhuhu"
SKIPS = (2, -2, 4)
SKIP_OF = (0, 0, 1, 1, 3, 3, 2, 2)
HELD_ROW = (0, 1) * (NZ // 2)


def skip_z(skip):
    return [(z, (z + skip) % NZ) for z in range(2)]


def ring_z(step):
    return [(z, (z + step) % NZ) for z in range(NZ)]


def one_hot_rows(order):
    source = lax.broadcasted_iota(jnp.int32, (B, B), 0)
    return jnp.where(source == order, 1.0, 0.0).T.astype(BF16)


def split(value, parts):
    out = []
    for _ in range(parts):
        head = value.astype(BF16)
        out.append(head)
        value = value - head.astype(F32)
    return out


def dot(a, b):
    return jnp.dot(a, b, preferred_element_type=F32)


def pack_kernel(pattern_hbm, order_hbm, blocks_hbm, packed_ref, first_ref, pattern, order, blocks, sem, block_sem):
    small = [
        pltpu.make_async_copy(order_hbm.at[0], order, sem.at[0]),
        pltpu.make_async_copy(pattern_hbm.at[0:8], pattern, sem.at[1]),
    ]
    fetches = [pltpu.make_async_copy(blocks_hbm.at[0, u], blocks.at[u], block_sem.at[u]) for u in range(LC)]
    for copy in small + fetches:
        copy.start()
    for copy in small:
        copy.wait()
    supernode = jnp.minimum(lax.axis_index("prow"), 1)
    grid_col = lax.axis_index("pcol")
    pick = one_hot_rows(order[...])
    slot = jnp.int32(0)
    chosen = [jnp.int32(0)] * UCAP
    for u in range(LC):
        col = grid_col + u * COLS_GRID
        used = (pattern[supernode, col] != 0) & (col > supernode)
        chosen = [jnp.where(used & (slot == s), u, c) for s, c in enumerate(chosen)]
        slot = slot + used.astype(jnp.int32)
    for copy in fetches:
        copy.wait()
    present = pattern[supernode, grid_col] != 0
    first_ref[...] = jnp.where(present, dot(pick, blocks[0]), 0.0).astype(BF16)
    for s, u in enumerate(chosen):
        block = dot(pick, blocks[u]).astype(BF16)
        for piece in range(NX):
            packed_ref[piece, s] = block[piece * PIECE : (piece + 1) * PIECE]


def permute_kernel(
    pattern_hbm, order_hbm, blocks_hbm, after, placed_ref, out_hbm, pattern, orders, blocks, sem, pattern_sem, block_sem, out_sem
):
    del after
    grid_row = lax.axis_index("prow")
    grid_col = lax.axis_index("pcol")
    small = [pltpu.make_async_copy(order_hbm, orders, sem)]
    for t in range(LR):
        group = pl.ds(pl.multiple_of((t * ROWS_GRID + grid_row) // 8 * 8, 8), 8)
        small.append(pltpu.make_async_copy(pattern_hbm.at[group], pattern.at[t], pattern_sem.at[t]))

    def fetch(t):
        return pltpu.make_async_copy(blocks_hbm.at[t], blocks.at[t], block_sem.at[t])

    def store(t):
        return pltpu.make_async_copy(placed_ref.at[t], out_hbm.at[t], out_sem.at[t])

    for copy in small:
        copy.start()
    for t in range(LR):
        fetch(t).start()
    for copy in small:
        copy.wait()

    def block_row(t, carry):
        pick = one_hot_rows(orders[t])
        fetch(t).wait()
        for u in range(LC):
            present = pattern[t, grid_row % 8, grid_col + u * COLS_GRID] != 0
            placed_ref[t, u] = jnp.where(present, dot(pick, blocks[t, u]), 0.0).astype(BF16)
        store(t).start()
        return carry

    lax.fori_loop(0, LR, block_row, 0)
    for t in range(LR):
        store(t).wait()


def select_kernel(choices, *refs):
    *options, out_ref = refs
    part, table = choices
    grid_row = lax.axis_index("prow")
    place = {"x": grid_row // NZ, "z": grid_row % NZ, "y": lax.axis_index("pcol") // 2}[part]
    for i in range(max(table) + 1):
        hit = functools.reduce(jnp.logical_or, [place == p for p, choice in enumerate(table) if choice == i])

        @pl.when(hit)
        def _(i=i):
            out_ref[...] = options[i][...]


def inverse_kernel(
    held_ref, up_ref, down_ref, pattern_hbm, order_hbm, blocks_hbm, after,
    lower_ref, first_ref, high_ref, low_ref, column_ref,
    pattern, orders, blocks, sem, pattern_sem,
):
    del after
    grid_row = lax.axis_index("prow")
    grid_col = lax.axis_index("pcol")
    z = grid_row % NZ

    def chosen(table):
        def of(letter, ref):
            hit = functools.reduce(jnp.logical_or, [z == i for i in range(NZ) if table[i] == letter])
            return hit, ref

        (held, h), (up, u) = of("h", held_ref), of("u", up_ref)
        return jnp.where(
            held, h[...].astype(F32), jnp.where(up, u[...].astype(F32), down_ref[...].astype(F32))
        )

    @pl.when(grid_col < 2)
    def _():
        fetches = [
            pltpu.make_async_copy(order_hbm, orders, sem.at[0]),
            pltpu.make_async_copy(blocks_hbm.at[:, 0], blocks, sem.at[1]),
        ]
        for t in range(LR):
            group = pl.ds(pl.multiple_of((t * ROWS_GRID + grid_row) // 8 * 8, 8), 8)
            fetches.append(pltpu.make_async_copy(pattern_hbm.at[group], pattern.at[t], pattern_sem.at[t]))
        for copy in fetches:
            copy.start()
        first = chosen(FROM_0)
        first_ref[...] = first.astype(BF16)
        block = jnp.where(grid_col == 0, first, chosen(FROM_1))
        diagonal = lax.broadcasted_iota(jnp.int32, (B, B), 0) == lax.broadcasted_iota(jnp.int32, (B, B), 1)
        pivots = jnp.where(diagonal, block, 0.0)
        by_col = 1.0 / jnp.sum(pivots, axis=0, keepdims=True)
        by_row = 1.0 / jnp.sum(pivots, axis=1, keepdims=True)
        twice = jnp.where(diagonal, 2.0, 0.0)
        inverse = by_row * (twice - block * by_col)
        block16 = block.astype(BF16)
        for _ in range(NEWTON - 1):
            high, middle, low = split(inverse, 3)
            rest = twice - (dot(block16, high) + (dot(block16, middle) + dot(block16, low)))
            rest_high, rest_low = split(rest, 2)
            inverse = dot(high, rest_high) + (dot(high, rest_low) + dot(middle, rest_high))
        high, low = split(inverse, 2)
        high_ref[...] = high
        low_ref[...] = low
        for copy in fetches:
            copy.wait()
        for t in range(LR):
            present = pattern[t, grid_row % 8, grid_col] != 0
            column = jnp.where(present, dot(one_hot_rows(orders[t]), blocks[t]), 0.0).astype(BF16)
            column_ref[t] = column
            lower = dot(column, high) + dot(column, low)
            lower_ref[t] = jnp.where(t * ROWS_GRID + grid_row > 0, lower, 0.0).astype(BF16)


def second_kernel(own_ref, lower_ref, first_ref, high_ref, low_ref, column_ref, out_ref):
    grid_row = lax.axis_index("prow")

    @pl.when(lax.axis_index("pcol") == 0)
    def _():
        out_ref[...] = own_ref[...]

    @pl.when(lax.axis_index("pcol") == 1)
    def _():
        for t in range(LR):
            rest = (column_ref[t].astype(F32) - dot(lower_ref[t], first_ref[...])).astype(BF16)
            lower = dot(rest, high_ref[...]) + dot(rest, low_ref[...])
            out_ref[t] = jnp.where(t * ROWS_GRID + grid_row > 1, lower, 0.0).astype(BF16)


def schur_kernel(
    pattern_hbm, held0, held1, held2, held3, other01, other23, mine_ref, neighbour_ref, placed, current_hbm,
    out_hbm, pattern, upper, work, sem, upper_sem, out_sem,
):
    del current_hbm
    grid_row = lax.axis_index("prow")
    grid_col = lax.axis_index("pcol")
    x, z = grid_row // NZ, grid_row % NZ
    held_row = functools.reduce(jnp.logical_or, [z == i for i in range(NZ) if HELD_ROW[i]]).astype(jnp.int32)

    def plan(u):
        col = grid_col + u * COLS_GRID
        use0 = (pattern[0, col] != 0) & (col > 0)
        use1 = (pattern[1, col] != 0) & (col > 1)
        return use0, use1, use0 | use1 | (col < 2)

    def store(u):
        return pltpu.make_async_copy(work.at[u], out_hbm.at[:, u], out_sem.at[u])

    rows_of = pltpu.make_async_copy(pattern_hbm.at[0:8], pattern, sem)
    rows_of.start()
    operands = []
    for k, refs in ((held_row, (held0, held1, held2, held3)), (1 - held_row, [pair.at[i] for pair in (other01, other23) for i in range(2)])):
        for shift, ref in enumerate(refs):
            part = pl.ds(pl.multiple_of((x + NX - shift) % NX * PIECE, PIECE), PIECE)
            operands.append(pltpu.make_async_copy(ref, upper.at[k, :, part, :], upper_sem.at[len(operands)]))
    for copy in operands:
        copy.start()
    rows_of.wait()

    for copy in operands:
        copy.wait()

    def step(u, slots):
        use0, use1, touched = plan(u)
        slot0, slot1 = slots

        @pl.when(touched)
        def _():
            @pl.when(jnp.logical_not(use0))
            def _():
                for t in range(LR):
                    work[u, t] = placed[t, u]

            for k, used, slot in ((0, use0, slot0), (1, use1, slot1)):
                for parity, lower in ((k, mine_ref), (1 - k, neighbour_ref)):

                    @pl.when(used & (grid_col % 2 == parity))
                    def _(k=k, slot=slot, lower=lower):
                        for t in range(LR):
                            block = work[u, t] if k else placed[t, u]
                            work[u, t] = (block.astype(F32) - dot(lower[t], upper[k, slot])).astype(BF16)

            @pl.when((u == 0) & (grid_col < 2))
            def _():
                for t in range(LR):

                    @pl.when(t * ROWS_GRID + grid_row > grid_col)
                    def _(t=t):
                        work[0, t] = mine_ref[t]

            store(u).start()

        return slot0 + use0.astype(jnp.int32), slot1 + use1.astype(jnp.int32)

    lax.fori_loop(0, LC, step, (jnp.int32(0), jnp.int32(0)))

    def finish(u, carry):
        @pl.when(plan(u)[2])
        def _():
            store(u).wait()

        return carry

    lax.fori_loop(0, LC, finish, 0)


def pick_by(index, options):
    value = None
    for i, option in enumerate(options):
        if option is not None:
            value = option if value is None else jnp.where(index == i, option, value)
    return value


def on_cols(rows, cols):
    return [(a * COLS_GRID + c, b * COLS_GRID + c) for a, b in rows for c in cols]


def along_z(pairs):
    return [(x * NZ + a, x * NZ + b) for x in range(NX) for a, b in pairs]


def scattered(sent):
    return [sent[0]] + [lax.ppermute(sent[d], "prow", [(z, d * NZ + z) for z in range(2)]) for d in range(1, NX)]


def select(part, table, *options, after=()):
    return pl.pallas_call(
        functools.partial(select_kernel, (part, tuple(table))),
        out_shape=jax.ShapeDtypeStruct(options[0].shape, options[0].dtype),
        in_specs=[vmem()] * len(options) + [anywhere()] * len(after),
        out_specs=vmem(),
        compiler_params=params(8),
        cost_estimate=cost(0, SELECT_BYTES),
        name="select",
    )(*options, *after)


def whole_pairs(z_pairs):
    rows = [[(x * NZ + a, x * NZ + b) for x in range(NX) for a, b in pairs] for pairs in z_pairs]
    return on_cols(rows[0], (0, 1)) + on_cols(rows[1], (1,))


def spread_whole(first, x, after):
    axes = ("prow", "pcol")
    starts = [on_cols([(0, d * NZ)], (0, 1)) + on_cols([(1, d * NZ + 1)], (1,)) for d in range(1, NX)]
    mine = pick_by(x, [first] + [lax.ppermute(first, axes, pairs) for pairs in starts])
    far_up, far_down = (lax.ppermute(mine, axes, whole_pairs(p)) for p in (FAR_UP, FAR_DOWN))
    held = select("z", (0, 0, 0, 1, 1, 2, 2, 0), mine, far_up, far_down, after=after)
    up, down = (lax.ppermute(held, axes, whole_pairs(p)) for p in (NEAR_UP, NEAR_DOWN))
    return held, up, down


def gather_x(own):
    shifted = [[(r, (r + d * NZ) % ROWS_GRID) for r in range(ROWS_GRID)] for d in range(1, NX)]
    return [own] + [lax.ppermute(own, "prow", pairs) for pairs in shifted]


def vmem():
    return pl.BlockSpec(memory_space=pltpu.VMEM)


def hbm():
    return pl.BlockSpec(memory_space=pltpu.HBM)


def in_hbm(value):
    return pltpu.with_memory_space_constraint(value, pltpu.HBM)


def anywhere():
    return pl.BlockSpec(memory_space=pl.ANY)


def like(*shape):
    return jax.ShapeDtypeStruct(shape, BF16)


def params(limit):
    return pltpu.CompilerParams(vmem_limit_bytes=limit * MIB)


def cost(flops, moved):
    return pl.CostEstimate(flops=flops, bytes_accessed=moved, transcendentals=0)


def local(matrix, row_perm, block_pattern):
    grid_row = lax.axis_index("prow")
    grid_col = lax.axis_index("pcol")
    x, z = grid_row // NZ, grid_row % NZ
    blocks = in_hbm(jnp.transpose(matrix[0, :, :, 0], (0, 2, 1, 3)))
    orders = in_hbm(row_perm.reshape(LR, 1, B))
    block_pattern = in_hbm(block_pattern)
    block = B * B * 2
    small_scratch = [pltpu.SMEM((8, NB), jnp.int32), pltpu.VMEM((1, B), jnp.int32)]
    dma = pltpu.SemaphoreType.DMA

    packed, first = pl.pallas_call(
        pack_kernel,
        out_shape=(like(NX, UCAP, PIECE, B), like(B, B)),
        in_specs=[hbm(), hbm(), hbm()],
        out_specs=(vmem(), vmem()),
        scratch_shapes=small_scratch + [pltpu.VMEM((LC, B, B), BF16), dma((2,)), dma((LC,))],
        compiler_params=params(16),
        cost_estimate=cost(2 * 7 * B**3, 19 * block),
        name="pack",
    )(block_pattern, orders, blocks)

    mine = select("x", range(NX), *scattered([packed[d] for d in range(NX)]))
    held, up, down = spread_whole(first, x, (mine,))
    skipped = [lax.ppermute(mine, "prow", along_z(skip_z(skip))) for skip in SKIPS]
    held_row = select("z", SKIP_OF, mine, *skipped)
    held_rows = gather_x(held_row)
    other_rows = [
        lax.ppermute(jnp.stack(held_rows[i : i + 2]), "prow", along_z(ring_z(step))) for i, step in ((0, 1), (2, -1))
    ]

    lower0, first0, high, low, column = pl.pallas_call(
        inverse_kernel,
        out_shape=(like(LR, B, B), like(B, B), like(B, B), like(B, B), like(LR, B, B)),
        in_specs=[vmem(), vmem(), vmem(), hbm(), hbm(), hbm(), anywhere()],
        out_specs=(vmem(),) * 5,
        scratch_shapes=[
            pltpu.SMEM((LR, 8, NB), jnp.int32),
            pltpu.VMEM((LR, 1, B), jnp.int32),
            pltpu.VMEM((LR, B, B), BF16),
            dma((2,)),
            dma((LR,)),
        ],
        compiler_params=params(16),
        cost_estimate=cost(2 * 18 * B**3, 12 * block),
        name="inverse",
    )(held, up, down, block_pattern, orders, blocks, held_row)

    neighbour0 = lax.ppermute(lower0, "pcol", [(0, 1)])
    lower = pl.pallas_call(
        second_kernel,
        out_shape=like(LR, B, B),
        in_specs=[vmem()] * 6,
        out_specs=vmem(),
        compiler_params=params(16),
        cost_estimate=cost(2 * 9 * B**3, 12 * block),
        name="second",
    )(lower0, neighbour0, first0, high, low, column)

    placed, current = pl.pallas_call(
        permute_kernel,
        out_shape=(pltpu.VMEM((LR, LC, B, B), BF16), like(LR, LC, B, B)),
        in_specs=[hbm()] * 3 + [anywhere()],
        out_specs=(vmem(), hbm()),
        scratch_shapes=[
            pltpu.SMEM((LR, 8, NB), jnp.int32),
            pltpu.VMEM((LR, 1, B), jnp.int32),
            pltpu.VMEM((LR, LC, B, B), BF16),
            dma,
            dma((LR,)),
            dma((LR,)),
            dma((LR,)),
        ],
        compiler_params=params(16),
        cost_estimate=cost(2 * LR * LC * B**3, 2 * LR * LC * block),
        name="permute",
    )(block_pattern, orders, blocks, lower)
    got = [lax.ppermute(lower, "pcol", [(0, 2 * d), (1, 2 * d + 1)]) for d in (3, 1, 2)]
    lower_mine = select("y", (0, 2, 3, 1), lower, *got, after=(placed,))
    lower_neighbour = lax.ppermute(lower_mine, "pcol", [(c, c ^ 1) for c in range(COLS_GRID)])

    current = pl.pallas_call(
        schur_kernel,
        out_shape=like(LR, LC, B, B),
        in_specs=[hbm()] + [anywhere()] * (NX + 2) + [vmem()] * 3 + [hbm()],
        out_specs=hbm(),
        scratch_shapes=[
            pltpu.SMEM((8, NB), jnp.int32),
            pltpu.VMEM((2, UCAP, B, B), BF16),
            pltpu.VMEM((LC, LR, B, B), BF16),
            dma,
            dma((2 * NX,)),
            dma((LC,)),
        ],
        input_output_aliases={NX + 6: 0},
        compiler_params=params(24),
        cost_estimate=cost(2 * LR * 12 * B**3, 90 * block),
        name="schur",
    )(block_pattern, *held_rows, *other_rows, lower_mine, lower_neighbour, placed, current)
    return jnp.transpose(current, (0, 2, 1, 3)).reshape(matrix.shape)


def solution(mesh):
    placed = (P("prow", None, None, "pcol", None, None), P("prow", None, None), P())
    return jax.shard_map(
        local,
        mesh=mesh,
        in_specs=placed,
        out_specs=P("prow", None, None, "pcol", None, None),
        check_vma=False,
    )
```

profile of v0, /device:TPU:2, one launch (start us, length us, event | category | flops | bytes accessed | tf_op | source)
XLA Modules:
  0.0 72.0 jit_solution(14763387351078809610)
XLA Ops:
  0.0 2.0 %pack.1 = (bf16[4,6,64,256]{3,2,1,0:T(8,128)(2,1)S(1)}, bf16[256,256]{1,0:T(8,128)(2,1)S(1)}) custom-call(s32[96,96]{1,0:T(8,128)} %pattern_hbm.7, s32[3,1,256]{2,1,0:T(1,128)} %bitcast.28, bf16[3,12,256,256]{3,2,1,0:T(8,128)(2,1)} %bitcast.25), custom_call_target="tpu_custom_call" | custom-call | flops 234881024 | bytes 2490368 | tf_op jit(solution)/shard_map/pack/pallas_call | solution.py:387
  2.0 1.3 %collective-permute-start.13 = (bf16[256,256]{1,0:T(8,128)(2,1)S(1)}, bf16[256,256]{1,0:T(8,128)(2,1)S(1)}, u32[]{:S(2)}, u32[]{:S(2)}) collective-permute-start(bf16[256,256]{1,0:T(8,128)(2,1)S(1)} %get-tuple-element.15), channel_id=1, source_target_pairs={{0,64},{1,65},{9,73}} | collective-permute-start | bytes 393224 | tf_op jit(solution)/shard_map/ppermute | solution.py:336
  3.3 0.7 collective-permute-start.12
  4.0 0.7 collective-permute-start.11
  4.7 0.7 collective-permute-start.2
  5.4 0.7 collective-permute-start.1
  6.1 3.6 %collective-permute-done.13 = bf16[256,256]{1,0:T(8,128)(2,1)S(1)} collective-permute-done((bf16[256,256]{1,0:T(8,128)(2,1)S(1)}, bf16[256,256]{1,0:T(8,128)(2,1)S(1)}, u32[]{:S(2)}, u32[]{:S(2)}) %collective-permute-start.13) | collective-permute-done | bytes 131104 | tf_op jit(solution)/shard_map/ppermute | solution.py:336
  9.7 1.3 %collective-permute-start = (bf16[6,64,256]{2,1,0:T(8,128)(2,1)S(1)}, bf16[6,64,256]{2,1,0:T(8,128)(2,1)S(1)}, u32[]{:S(2)}, u32[]{:S(2)}) collective-permute-start(bf16[6,64,256]{2,1,0:T(8,128)(2,1)S(1)} %get-tuple-element.25), channel_id=1, source_target_pairs={{0,64},{8,72},{1,65},{9,73},{2,66},{10,74},{3,67},{11,75},{4,68},{... | collective-permute-start | bytes 589832 | tf_op jit(solution)/shard_map/ppermute | solution.py:313
  11.1 3.8 %collective-permute-start.15 = (bf16[256,256]{1,0:T(8,128)(2,1)S(1)}, bf16[256,256]{1,0:T(8,128)(2,1)S(1)}, u32[]{:S(2)}, u32[]{:S(2)}) collective-permute-start(bf16[256,256]{1,0:T(8,128)(2,1)S(1)} %select_select_fusion.refs_0_), channel_id=1, source_target_pairs={{0,40},{1,41},{64,104},{65,105},{128,168},{129,169},{192,232},{193... | collective-permute-start | bytes 393224 | tf_op jit(solution)/shard_map/ppermute | solution.py:337
  14.9 1.3 %collective-permute-start.14 = (bf16[256,256]{1,0:T(8,128)(2,1)S(1)}, bf16[256,256]{1,0:T(8,128)(2,1)S(1)}, u32[]{:S(2)}, u32[]{:S(2)}) collective-permute-start(bf16[256,256]{1,0:T(8,128)(2,1)S(1)} %select_select_fusion.refs_0_), channel_id=1, source_target_pairs={{0,24},{1,25},{64,88},{65,89},{128,152},{129,153},{192,216},{193,2... | collective-permute-start | bytes 393224 | tf_op jit(solution)/shard_map/ppermute | solution.py:337
  16.2 4.7 %collective-permute-done.refs_1_ = bf16[6,64,256]{2,1,0:T(8,128)(2,1)S(1)} collective-permute-done((bf16[6,64,256]{2,1,0:T(8,128)(2,1)S(1)}, bf16[6,64,256]{2,1,0:T(8,128)(2,1)S(1)}, u32[]{:S(2)}, u32[]{:S(2)}) %collective-permute-start) | collective-permute-done | bytes 196640 | tf_op jit(solution)/shard_map/ppermute | solution.py:313
  21.0 1.3 %collective-permute-start.5 = (bf16[6,64,256]{2,1,0:T(8,128)(2,1)S(1)}, bf16[6,64,256]{2,1,0:T(8,128)(2,1)S(1)}, u32[]{:S(2)}, u32[]{:S(2)}) collective-permute-start(bf16[6,64,256]{2,1,0:T(8,128)(2,1)S(1)} %select.8.refs_0_.refs_3_), channel_id=1, source_target_pairs={{0,32},{8,40},{64,96},{72,104},{128,160},{136,168},{192,224},{200,... | collective-permute-start | bytes 589832 | tf_op jit(solution)/shard_map/ppermute | solution.py:400
  22.3 1.3 %collective-permute-start.4 = (bf16[6,64,256]{2,1,0:T(8,128)(2,1)S(1)}, bf16[6,64,256]{2,1,0:T(8,128)(2,1)S(1)}, u32[]{:S(2)}, u32[]{:S(2)}) collective-permute-start(bf16[6,64,256]{2,1,0:T(8,128)(2,1)S(1)} %select.8.refs_0_.refs_3_), channel_id=1, source_target_pairs={{0,48},{8,56},{64,112},{72,120},{128,176},{136,184},{192,240},{200... | collective-permute-start | bytes 589832 | tf_op jit(solution)/shard_map/ppermute | solution.py:400
  23.6 1.3 %collective-permute-start.3 = (bf16[6,64,256]{2,1,0:T(8,128)(2,1)S(1)}, bf16[6,64,256]{2,1,0:T(8,128)(2,1)S(1)}, u32[]{:S(2)}, u32[]{:S(2)}) collective-permute-start(bf16[6,64,256]{2,1,0:T(8,128)(2,1)S(1)} %select.8.refs_0_.refs_3_), channel_id=1, source_target_pairs={{0,16},{8,24},{64,80},{72,88},{128,144},{136,152},{192,208},{200,2... | collective-permute-start | bytes 589832 | tf_op jit(solution)/shard_map/ppermute | solution.py:400
  24.9 1.3 %collective-permute-start.17 = (bf16[256,256]{1,0:T(8,128)(2,1)S(1)}, bf16[256,256]{1,0:T(8,128)(2,1)S(1)}, u32[]{:S(2)}, u32[]{:S(2)}) collective-permute-start(bf16[256,256]{1,0:T(8,128)(2,1)S(1)} %select.10.held_ref), channel_id=1, source_target_pairs={{0,56},{1,57},{24,16},{25,17},{64,120},{65,121},{88,80},{89,81},{1... | collective-permute-start | bytes 393224 | tf_op jit(solution)/shard_map/ppermute | solution.py:339
  26.3 2.5 %collective-permute-start.16 = (bf16[256,256]{1,0:T(8,128)(2,1)S(1)}, bf16[256,256]{1,0:T(8,128)(2,1)S(1)}, u32[]{:S(2)}, u32[]{:S(2)}) collective-permute-start(bf16[256,256]{1,0:T(8,128)(2,1)S(1)} %select.10.held_ref), channel_id=1, source_target_pairs={{0,8},{1,9},{24,32},{25,33},{40,48},{41,49},{64,72},{65,73},{88,96... | collective-permute-start | bytes 393224 | tf_op jit(solution)/shard_map/ppermute | solution.py:339
  28.8 7.4 %collective-permute-done.4.refs_2_ = bf16[6,64,256]{2,1,0:T(8,128)(2,1)S(1)} collective-permute-done((bf16[6,64,256]{2,1,0:T(8,128)(2,1)S(1)}, bf16[6,64,256]{2,1,0:T(8,128)(2,1)S(1)}, u32[]{:S(2)}, u32[]{:S(2)}) %collective-permute-start.4) | collective-permute-done | bytes 196640 | tf_op jit(solution)/shard_map/ppermute | solution.py:400
  36.2 2.1 %collective-permute-done.17.down_ref = bf16[256,256]{1,0:T(8,128)(2,1)S(1)} collective-permute-done((bf16[256,256]{1,0:T(8,128)(2,1)S(1)}, bf16[256,256]{1,0:T(8,128)(2,1)S(1)}, u32[]{:S(2)}, u32[]{:S(2)}) %collective-permute-start.17) | collective-permute-done | bytes 131104 | tf_op jit(solution)/shard_map/ppermute | solution.py:339
  38.3 2.3 %inverse.1 = (bf16[3,256,256]{2,1,0:T(8,128)(2,1)S(1)}, bf16[256,256]{1,0:T(8,128)(2,1)S(1)}, bf16[256,256]{1,0:T(8,128)(2,1)S(1)}, bf16[256,256]{1,0:T(8,128)(2,1)S(1)}, bf16[3,256,256]{2,1,0:T(8,128)(2,1)S(1)}) custom-call(bf16[256,256]{1,0:T(8,128)(2,1)S(1)} %select.10.held_ref, bf16[256,256]{1,0:T(8,128)(2,1)S(1)} %collective-permute-done.16.up_ref, ...), custom_call_target="tpu_custom_call" | custom-call | flops 603979776 | bytes 1572864 | tf_op jit(solution)/shard_map/inverse/pallas_call | solution.py:407
  40.7 1.4 %collective-permute-start.18 = (bf16[3,256,256]{2,1,0:T(8,128)(2,1)S(1)}, bf16[3,256,256]{2,1,0:T(8,128)(2,1)S(1)}, u32[]{:S(2)}, u32[]{:S(2)}) collective-permute-start(bf16[3,256,256]{2,1,0:T(8,128)(2,1)S(1)} %get-tuple-element.16.own_ref), channel_id=1, source_target_pairs={{0,1},{8,9},{16,17},{24,25},{32,33},{40,41},{48,49},{56,57},{64,65... | collective-permute-start | bytes 1179656 | tf_op jit(solution)/shard_map/ppermute | solution.py:424
  42.1 0.7 collective-permute-start.7
  42.8 1.8 %collective-permute-start.6 = (bf16[6,64,256]{2,1,0:T(8,128)(2,1)S(1)}, bf16[6,64,256]{2,1,0:T(8,128)(2,1)S(1)}, u32[]{:S(2)}, u32[]{:S(2)}) collective-permute-start(bf16[6,64,256]{2,1,0:T(8,128)(2,1)S(1)} %select.9.after.held0), channel_id=1, source_target_pairs={{0,64},{8,72},{16,80},{24,88},{32,96},{40,104},{48,112},{56,120},{... | collective-permute-start | bytes 589832 | tf_op jit(solution)/shard_map/ppermute | solution.py:345
  44.7 1.3 %collective-permute-start.21 = (bf16[3,256,256]{2,1,0:T(8,128)(2,1)S(1)}, bf16[3,256,256]{2,1,0:T(8,128)(2,1)S(1)}, u32[]{:S(2)}, u32[]{:S(2)}) collective-permute-start(bf16[3,256,256]{2,1,0:T(8,128)(2,1)S(1)} %second.1.after.refs_0_), channel_id=1, source_target_pairs={{0,4},{1,5},{8,12},{9,13},{16,20},{17,21},{24,28},{25,29},{32,36},... | collective-permute-start | bytes 1179656 | tf_op jit(solution)/shard_map/ppermute | solution.py:453
  46.0 1.3 %collective-permute-start.20 = (bf16[3,256,256]{2,1,0:T(8,128)(2,1)S(1)}, bf16[3,256,256]{2,1,0:T(8,128)(2,1)S(1)}, u32[]{:S(2)}, u32[]{:S(2)}) collective-permute-start(bf16[3,256,256]{2,1,0:T(8,128)(2,1)S(1)} %second.1.after.refs_0_), channel_id=1, source_target_pairs={{0,2},{1,3},{8,10},{9,11},{16,18},{17,19},{24,26},{25,27},{32,34},... | collective-permute-start | bytes 1179656 | tf_op jit(solution)/shard_map/ppermute | solution.py:453
  47.3 5.2 %collective-permute-done.8.held3 = bf16[6,64,256]{2,1,0:T(8,128)(2,1)S(1)} collective-permute-done((bf16[6,64,256]{2,1,0:T(8,128)(2,1)S(1)}, bf16[6,64,256]{2,1,0:T(8,128)(2,1)S(1)}, u32[]{:S(2)}, u32[]{:S(2)}) %collective-permute-start.8) | collective-permute-done | bytes 196640 | tf_op jit(solution)/shard_map/ppermute | solution.py:345
  52.5 1.3 %collective-permute-start.19 = (bf16[3,256,256]{2,1,0:T(8,128)(2,1)S(1)}, bf16[3,256,256]{2,1,0:T(8,128)(2,1)S(1)}, u32[]{:S(2)}, u32[]{:S(2)}) collective-permute-start(bf16[3,256,256]{2,1,0:T(8,128)(2,1)S(1)} %second.1.after.refs_0_), channel_id=1, source_target_pairs={{0,6},{1,7},{8,14},{9,15},{16,22},{17,23},{24,30},{25,31},{32,38},... | collective-permute-start | bytes 1179656 | tf_op jit(solution)/shard_map/ppermute | solution.py:453
  53.9 3.8 %collective-permute-start.10 = (bf16[2,6,64,256]{3,2,1,0:T(8,128)(2,1)S(1)}, bf16[2,6,64,256]{3,2,1,0:T(8,128)(2,1)S(1)}, u32[]{:S(2)}, u32[]{:S(2)}) collective-permute-start(bf16[2,6,64,256]{3,2,1,0:T(8,128)(2,1)S(1)} %pad_maximum_fusion.1), channel_id=1, source_target_pairs={{0,56},{8,0},{16,8},{24,16},{32,24},{40,32},{48,40},{56,48},{64,12... | collective-permute-start | bytes 1179656 | tf_op jit(solution)/shard_map/ppermute | solution.py:404
  57.8 5.0 %permute.1 = (bf16[3,12,256,256]{3,2,1,0:T(8,128)(2,1)S(1)}, bf16[3,12,256,256]{3,2,1,0:T(8,128)(2,1)}) custom-call(s32[96,96]{1,0:T(8,128)} %pattern_hbm.7, s32[3,1,256]{2,1,0:T(1,128)} %bitcast.30, bf16[3,12,256,256]{3,2,1,0:T(8,128)(2,1)} %bitcast.27, bf16[3,256,256]{2,1,0:T(8,128)(2,1)S(1)} %second.1.after.refs_0_), custom_call_target="tpu_custom_call" | custom-call | flops 1207959552 | bytes 9437184 | tf_op jit(solution)/shard_map/permute/pallas_call | solution.py:435
  62.8 0.1 collective-permute-done.20.refs_2_
  63.1 1.5 %collective-permute-done.10.other23 = bf16[2,6,64,256]{3,2,1,0:T(8,128)(2,1)S(1)} collective-permute-done((bf16[2,6,64,256]{3,2,1,0:T(8,128)(2,1)S(1)}, bf16[2,6,64,256]{3,2,1,0:T(8,128)(2,1)S(1)}, u32[]{:S(2)}, u32[]{:S(2)}) %collective-permute-start.10) | collective-permute-done | bytes 393248 | tf_op jit(solution)/shard_map/ppermute | solution.py:404
  64.6 3.5 %collective-permute-done.9.other01 = bf16[2,6,64,256]{3,2,1,0:T(8,128)(2,1)S(1)} collective-permute-done((bf16[2,6,64,256]{3,2,1,0:T(8,128)(2,1)S(1)}, bf16[2,6,64,256]{3,2,1,0:T(8,128)(2,1)S(1)}, u32[]{:S(2)}, u32[]{:S(2)}) %collective-permute-start.9) | collective-permute-done | bytes 393248 | tf_op jit(solution)/shard_map/ppermute | solution.py:404
  68.2 3.8 %schur.1 = bf16[3,12,256,256]{3,2,1,0:T(8,128)(2,1)} custom-call(s32[96,96]{1,0:T(8,128)} %pattern_hbm.7, bf16[6,64,256]{2,1,0:T(8,128)(2,1)S(1)} %select.9.after.held0, bf16[6,64,256]{2,1,0:T(8,128)(2,1)S(1)} %collective-permute-done.6.held1, bf16[6,64,256]{2,1,0:T(8,128)(2,1)S(1)} %collective-permute-done.7.held2, ...), custom_call_target="tpu_custom_call", output_to_operand_aliasing={{}: (10, {})} | custom-call | flops 1207959552 | bytes 11796480 | tf_op jit(solution)/shard_map/schur/pallas_call | solution.py:457
  (27 shorter events, 0.6 us)
Async XLA Ops:
  2.0 7.7 %collective-permute-start.13 = (bf16[256,256]{1,0:T(8,128)(2,1)S(1)}, bf16[256,256]{1,0:T(8,128)(2,1)S(1)}, u32[]{:S(2)}, u32[]{:S(2)}) collective-permute-start(bf16[256,256]{1,0:T(8,128)(2,1)S(1)} %get-tuple-element.15), channel_id=1, source_target_pairs={{0,64},{1,65},{9,73}} | collective-permute-start | bytes 393224 | tf_op jit(solution)/shard_map/ppermute | solution.py:336
  3.3 7.7 %collective-permute-start.12 = (bf16[256,256]{1,0:T(8,128)(2,1)S(1)}, bf16[256,256]{1,0:T(8,128)(2,1)S(1)}, u32[]{:S(2)}, u32[]{:S(2)}) collective-permute-start(bf16[256,256]{1,0:T(8,128)(2,1)S(1)} %get-tuple-element.15), channel_id=1, source_target_pairs={{0,128},{1,129},{9,137}} | collective-permute-start | bytes 393224 | tf_op jit(solution)/shard_map/ppermute | solution.py:336
  4.0 7.0 %collective-permute-start.11 = (bf16[256,256]{1,0:T(8,128)(2,1)S(1)}, bf16[256,256]{1,0:T(8,128)(2,1)S(1)}, u32[]{:S(2)}, u32[]{:S(2)}) collective-permute-start(bf16[256,256]{1,0:T(8,128)(2,1)S(1)} %get-tuple-element.15), channel_id=1, source_target_pairs={{0,192},{1,193},{9,201}} | collective-permute-start | bytes 393224 | tf_op jit(solution)/shard_map/ppermute | solution.py:336
  4.7 11.5 %collective-permute-start.2 = (bf16[6,64,256]{2,1,0:T(8,128)(2,1)S(1)}, bf16[6,64,256]{2,1,0:T(8,128)(2,1)S(1)}, u32[]{:S(2)}, u32[]{:S(2)}) collective-permute-start(bf16[6,64,256]{2,1,0:T(8,128)(2,1)S(1)} %get-tuple-element.23), channel_id=1, source_target_pairs={{0,192},{8,200},{1,193},{9,201},{2,194},{10,202},{3,195},{11,203},... | collective-permute-start | bytes 589832 | tf_op jit(solution)/shard_map/ppermute | solution.py:313
  5.4 10.8 %collective-permute-start.1 = (bf16[6,64,256]{2,1,0:T(8,128)(2,1)S(1)}, bf16[6,64,256]{2,1,0:T(8,128)(2,1)S(1)}, u32[]{:S(2)}, u32[]{:S(2)}) collective-permute-start(bf16[6,64,256]{2,1,0:T(8,128)(2,1)S(1)} %get-tuple-element.24), channel_id=1, source_target_pairs={{0,128},{8,136},{1,129},{9,137},{2,130},{10,138},{3,131},{11,139},... | collective-permute-start | bytes 589832 | tf_op jit(solution)/shard_map/ppermute | solution.py:313
  9.7 11.2 %collective-permute-start = (bf16[6,64,256]{2,1,0:T(8,128)(2,1)S(1)}, bf16[6,64,256]{2,1,0:T(8,128)(2,1)S(1)}, u32[]{:S(2)}, u32[]{:S(2)}) collective-permute-start(bf16[6,64,256]{2,1,0:T(8,128)(2,1)S(1)} %get-tuple-element.25), channel_id=1, source_target_pairs={{0,64},{8,72},{1,65},{9,73},{2,66},{10,74},{3,67},{11,75},{4,68},{... | collective-permute-start | bytes 589832 | tf_op jit(solution)/shard_map/ppermute | solution.py:313
  11.1 13.8 %collective-permute-start.15 = (bf16[256,256]{1,0:T(8,128)(2,1)S(1)}, bf16[256,256]{1,0:T(8,128)(2,1)S(1)}, u32[]{:S(2)}, u32[]{:S(2)}) collective-permute-start(bf16[256,256]{1,0:T(8,128)(2,1)S(1)} %select_select_fusion.refs_0_), channel_id=1, source_target_pairs={{0,40},{1,41},{64,104},{65,105},{128,168},{129,169},{192,232},{193... | collective-permute-start | bytes 393224 | tf_op jit(solution)/shard_map/ppermute | solution.py:337
  14.9 10.0 %collective-permute-start.14 = (bf16[256,256]{1,0:T(8,128)(2,1)S(1)}, bf16[256,256]{1,0:T(8,128)(2,1)S(1)}, u32[]{:S(2)}, u32[]{:S(2)}) collective-permute-start(bf16[256,256]{1,0:T(8,128)(2,1)S(1)} %select_select_fusion.refs_0_), channel_id=1, source_target_pairs={{0,24},{1,25},{64,88},{65,89},{128,152},{129,153},{192,216},{193,2... | collective-permute-start | bytes 393224 | tf_op jit(solution)/shard_map/ppermute | solution.py:337
  21.0 7.8 %collective-permute-start.5 = (bf16[6,64,256]{2,1,0:T(8,128)(2,1)S(1)}, bf16[6,64,256]{2,1,0:T(8,128)(2,1)S(1)}, u32[]{:S(2)}, u32[]{:S(2)}) collective-permute-start(bf16[6,64,256]{2,1,0:T(8,128)(2,1)S(1)} %select.8.refs_0_.refs_3_), channel_id=1, source_target_pairs={{0,32},{8,40},{64,96},{72,104},{128,160},{136,168},{192,224},{200,... | collective-permute-start | bytes 589832 | tf_op jit(solution)/shard_map/ppermute | solution.py:400
  22.3 13.9 %collective-permute-start.4 = (bf16[6,64,256]{2,1,0:T(8,128)(2,1)S(1)}, bf16[6,64,256]{2,1,0:T(8,128)(2,1)S(1)}, u32[]{:S(2)}, u32[]{:S(2)}) collective-permute-start(bf16[6,64,256]{2,1,0:T(8,128)(2,1)S(1)} %select.8.refs_0_.refs_3_), channel_id=1, source_target_pairs={{0,48},{8,56},{64,112},{72,120},{128,176},{136,184},{192,240},{200... | collective-permute-start | bytes 589832 | tf_op jit(solution)/shard_map/ppermute | solution.py:400
  23.6 12.6 %collective-permute-start.3 = (bf16[6,64,256]{2,1,0:T(8,128)(2,1)S(1)}, bf16[6,64,256]{2,1,0:T(8,128)(2,1)S(1)}, u32[]{:S(2)}, u32[]{:S(2)}) collective-permute-start(bf16[6,64,256]{2,1,0:T(8,128)(2,1)S(1)} %select.8.refs_0_.refs_3_), channel_id=1, source_target_pairs={{0,16},{8,24},{64,80},{72,88},{128,144},{136,152},{192,208},{200,2... | collective-permute-start | bytes 589832 | tf_op jit(solution)/shard_map/ppermute | solution.py:400
  24.9 13.4 %collective-permute-start.17 = (bf16[256,256]{1,0:T(8,128)(2,1)S(1)}, bf16[256,256]{1,0:T(8,128)(2,1)S(1)}, u32[]{:S(2)}, u32[]{:S(2)}) collective-permute-start(bf16[256,256]{1,0:T(8,128)(2,1)S(1)} %select.10.held_ref), channel_id=1, source_target_pairs={{0,56},{1,57},{24,16},{25,17},{64,120},{65,121},{88,80},{89,81},{1... | collective-permute-start | bytes 393224 | tf_op jit(solution)/shard_map/ppermute | solution.py:339
  26.3 12.1 %collective-permute-start.16 = (bf16[256,256]{1,0:T(8,128)(2,1)S(1)}, bf16[256,256]{1,0:T(8,128)(2,1)S(1)}, u32[]{:S(2)}, u32[]{:S(2)}) collective-permute-start(bf16[256,256]{1,0:T(8,128)(2,1)S(1)} %select.10.held_ref), channel_id=1, source_target_pairs={{0,8},{1,9},{24,32},{25,33},{40,48},{41,49},{64,72},{65,73},{88,96... | collective-permute-start | bytes 393224 | tf_op jit(solution)/shard_map/ppermute | solution.py:339
  40.7 4.0 %collective-permute-start.18 = (bf16[3,256,256]{2,1,0:T(8,128)(2,1)S(1)}, bf16[3,256,256]{2,1,0:T(8,128)(2,1)S(1)}, u32[]{:S(2)}, u32[]{:S(2)}) collective-permute-start(bf16[3,256,256]{2,1,0:T(8,128)(2,1)S(1)} %get-tuple-element.16.own_ref), channel_id=1, source_target_pairs={{0,1},{8,9},{16,17},{24,25},{32,33},{40,41},{48,49},{56,57},{64,65... | collective-permute-start | bytes 1179656 | tf_op jit(solution)/shard_map/ppermute | solution.py:424
  42.0 10.5 %collective-permute-start.8 = (bf16[6,64,256]{2,1,0:T(8,128)(2,1)S(1)}, bf16[6,64,256]{2,1,0:T(8,128)(2,1)S(1)}, u32[]{:S(2)}, u32[]{:S(2)}) collective-permute-start(bf16[6,64,256]{2,1,0:T(8,128)(2,1)S(1)} %select.9.after.held0), channel_id=1, source_target_pairs={{0,192},{8,200},{16,208},{24,216},{32,224},{40,232},{48,240},{56,2... | collective-permute-start | bytes 589832 | tf_op jit(solution)/shard_map/ppermute | solution.py:345
  42.1 11.7 %collective-permute-start.7 = (bf16[6,64,256]{2,1,0:T(8,128)(2,1)S(1)}, bf16[6,64,256]{2,1,0:T(8,128)(2,1)S(1)}, u32[]{:S(2)}, u32[]{:S(2)}) collective-permute-start(bf16[6,64,256]{2,1,0:T(8,128)(2,1)S(1)} %select.9.after.held0), channel_id=1, source_target_pairs={{0,128},{8,136},{16,144},{24,152},{32,160},{40,168},{48,176},{56,1... | collective-permute-start | bytes 589832 | tf_op jit(solution)/shard_map/ppermute | solution.py:345
  42.8 14.8 %collective-permute-start.6 = (bf16[6,64,256]{2,1,0:T(8,128)(2,1)S(1)}, bf16[6,64,256]{2,1,0:T(8,128)(2,1)S(1)}, u32[]{:S(2)}, u32[]{:S(2)}) collective-permute-start(bf16[6,64,256]{2,1,0:T(8,128)(2,1)S(1)} %select.9.after.held0), channel_id=1, source_target_pairs={{0,64},{8,72},{16,80},{24,88},{32,96},{40,104},{48,112},{56,120},{... | collective-permute-start | bytes 589832 | tf_op jit(solution)/shard_map/ppermute | solution.py:345
  44.7 18.1 %collective-permute-start.21 = (bf16[3,256,256]{2,1,0:T(8,128)(2,1)S(1)}, bf16[3,256,256]{2,1,0:T(8,128)(2,1)S(1)}, u32[]{:S(2)}, u32[]{:S(2)}) collective-permute-start(bf16[3,256,256]{2,1,0:T(8,128)(2,1)S(1)} %second.1.after.refs_0_), channel_id=1, source_target_pairs={{0,4},{1,5},{8,12},{9,13},{16,20},{17,21},{24,28},{25,29},{32,36},... | collective-permute-start | bytes 1179656 | tf_op jit(solution)/shard_map/ppermute | solution.py:453
  46.0 16.9 %collective-permute-start.20 = (bf16[3,256,256]{2,1,0:T(8,128)(2,1)S(1)}, bf16[3,256,256]{2,1,0:T(8,128)(2,1)S(1)}, u32[]{:S(2)}, u32[]{:S(2)}) collective-permute-start(bf16[3,256,256]{2,1,0:T(8,128)(2,1)S(1)} %second.1.after.refs_0_), channel_id=1, source_target_pairs={{0,2},{1,3},{8,10},{9,11},{16,18},{17,19},{24,26},{25,27},{32,34},... | collective-permute-start | bytes 1179656 | tf_op jit(solution)/shard_map/ppermute | solution.py:453
  52.5 10.4 %collective-permute-start.19 = (bf16[3,256,256]{2,1,0:T(8,128)(2,1)S(1)}, bf16[3,256,256]{2,1,0:T(8,128)(2,1)S(1)}, u32[]{:S(2)}, u32[]{:S(2)}) collective-permute-start(bf16[3,256,256]{2,1,0:T(8,128)(2,1)S(1)} %second.1.after.refs_0_), channel_id=1, source_target_pairs={{0,6},{1,7},{8,14},{9,15},{16,22},{17,23},{24,30},{25,31},{32,38},... | collective-permute-start | bytes 1179656 | tf_op jit(solution)/shard_map/ppermute | solution.py:453
  53.9 10.7 %collective-permute-start.10 = (bf16[2,6,64,256]{3,2,1,0:T(8,128)(2,1)S(1)}, bf16[2,6,64,256]{3,2,1,0:T(8,128)(2,1)S(1)}, u32[]{:S(2)}, u32[]{:S(2)}) collective-permute-start(bf16[2,6,64,256]{3,2,1,0:T(8,128)(2,1)S(1)} %pad_maximum_fusion.1), channel_id=1, source_target_pairs={{0,56},{8,0},{16,8},{24,16},{32,24},{40,32},{48,40},{56,48},{64,12... | collective-permute-start | bytes 1179656 | tf_op jit(solution)/shard_map/ppermute | solution.py:404
  57.7 10.5 %collective-permute-start.9 = (bf16[2,6,64,256]{3,2,1,0:T(8,128)(2,1)S(1)}, bf16[2,6,64,256]{3,2,1,0:T(8,128)(2,1)S(1)}, u32[]{:S(2)}, u32[]{:S(2)}) collective-permute-start(bf16[2,6,64,256]{3,2,1,0:T(8,128)(2,1)S(1)} %pad_maximum_fusion), channel_id=1, source_target_pairs={{0,8},{8,16},{16,24},{24,32},{32,40},{40,48},{48,56},{56,0},{64,72... | collective-permute-start | bytes 1179656 | tf_op jit(solution)/shard_map/ppermute | solution.py:404
  63.0 5.2 %collective-permute-start.22 = (bf16[3,256,256]{2,1,0:T(8,128)(2,1)S(1)}, bf16[3,256,256]{2,1,0:T(8,128)(2,1)S(1)}, u32[]{:S(2)}, u32[]{:S(2)}) collective-permute-start(bf16[3,256,256]{2,1,0:T(8,128)(2,1)S(1)} %select.11.mine_ref), channel_id=1, source_target_pairs={{0,1},{1,0},{2,3},{3,2},{4,5},{5,4},{6,7},{7,6},{8,9},{9,8},{10,11... | collective-permute-start | bytes 1179656 | tf_op jit(solution)/shard_map/ppermute | solution.py:455
where the time goes:
time: 72.3 us; the launch traced here: 72 us
  starting transfers between devices  29.9 us (41%)
  waiting for transfers between devices  28.3 us (39%)
  Pallas kernels  13.3 us (18%)
    ppermute x3, waiting for transfers between devices, local(): lax.ppermute(mine, 'prow', along_z(skip_z(skip)))  7.43 us
    ppermute x3, waiting for transfers between devices, gather_x(): return [own] + [lax.ppermute(own, 'prow', pairs) for pairs in shifted]  5.18 us
    ppermute x2, starting transfers between devices, spread_whole(): lax.ppermute(mine, axes, whole_pairs(p))  5.11 us
    ppermute x2, waiting for transfers between devices, local(): lax.ppermute(jnp.stack(held_rows[i:i + 2]), 'prow', along_z(ring_z(step)))  5.08 us
    pallas_call x1, Pallas kernels, local(): pl.pallas_call(permute_kernel, out_shape=(pltpu.VMEM((LR, LC, B, B), BF16...  5.01 us
    ppermute x3, waiting for transfers between devices, scattered(): lax.ppermute(sent[d], 'prow', [(z, d * NZ + z) for z in range(2)])  4.73 us
    ppermute x3, starting transfers between devices, local(): lax.ppermute(lower, 'pcol', [(0, 2 * d), (1, 2 * d + 1)])  3.93 us
    ppermute x3, starting transfers between devices, local(): lax.ppermute(mine, 'prow', along_z(skip_z(skip)))  3.9 us
  transfers between devices with their start and end apart: 23, of which 8 were waited for; matrix products, arithmetic and copies ran while one was open for 0% of the time, Pallas kernels for 7%

commit v1 on v0

--- a/solution.py
+++ b/solution.py
@@ -92,7 +92,7 @@
 
 
 def permute_kernel(
-    pattern_hbm, order_hbm, blocks_hbm, after, placed_ref, out_hbm, pattern, orders, blocks, sem, pattern_sem, block_sem, out_sem
+    pattern_hbm, order_hbm, blocks_hbm, after, placed_ref, pattern, orders, blocks, sem, pattern_sem, block_sem
 ):
     del after
     grid_row = lax.axis_index("prow")
@@ -104,9 +104,6 @@
 
     def fetch(t):
         return pltpu.make_async_copy(blocks_hbm.at[t], blocks.at[t], block_sem.at[t])
-
-    def store(t):
-        return pltpu.make_async_copy(placed_ref.at[t], out_hbm.at[t], out_sem.at[t])
 
     for copy in small:
         copy.start()
@@ -121,12 +118,9 @@
         for u in range(LC):
             present = pattern[t, grid_row % 8, grid_col + u * COLS_GRID] != 0
             placed_ref[t, u] = jnp.where(present, dot(pick, blocks[t, u]), 0.0).astype(BF16)
-        store(t).start()
         return carry
 
     lax.fori_loop(0, LR, block_row, 0)
-    for t in range(LR):
-        store(t).wait()
 
 
 def select_kernel(choices, *refs):
@@ -217,10 +211,9 @@
 
 
 def schur_kernel(
-    pattern_hbm, held0, held1, held2, held3, other01, other23, mine_ref, neighbour_ref, placed, current_hbm,
+    pattern_hbm, held0, held1, held2, held3, other01, other23, mine_ref, neighbour_ref, placed,
     out_hbm, pattern, upper, work, sem, upper_sem, out_sem,
 ):
-    del current_hbm
     grid_row = lax.axis_index("prow")
     grid_col = lax.axis_index("pcol")
     x, z = grid_row // NZ, grid_row % NZ
@@ -234,6 +227,9 @@
 
     def store(u):
         return pltpu.make_async_copy(work.at[u], out_hbm.at[:, u], out_sem.at[u])
+
+    def passed(u):
+        return pltpu.make_async_copy(placed.at[:, u], out_hbm.at[:, u], out_sem.at[u])
 
     rows_of = pltpu.make_async_copy(pattern_hbm.at[0:8], pattern, sem)
     rows_of.start()
@@ -246,6 +242,14 @@
         copy.start()
     rows_of.wait()
 
+    def start_passed(u, carry):
+        @pl.when(jnp.logical_not(plan(u)[2]))
+        def _():
+            passed(u).start()
+
+        return carry
+
+    lax.fori_loop(0, LC, start_passed, 0)
     for copy in operands:
         copy.wait()
 
@@ -284,10 +288,7 @@
     lax.fori_loop(0, LC, step, (jnp.int32(0), jnp.int32(0)))
 
     def finish(u, carry):
-        @pl.when(plan(u)[2])
-        def _():
-            store(u).wait()
-
+        store(u).wait()
         return carry
 
     lax.fori_loop(0, LC, finish, 0)
@@ -432,17 +433,16 @@
         name="second",
     )(lower0, neighbour0, first0, high, low, column)
 
-    placed, current = pl.pallas_call(
+    placed = pl.pallas_call(
         permute_kernel,
-        out_shape=(pltpu.VMEM((LR, LC, B, B), BF16), like(LR, LC, B, B)),
+        out_shape=pltpu.VMEM((LR, LC, B, B), BF16),
         in_specs=[hbm()] * 3 + [anywhere()],
-        out_specs=(vmem(), hbm()),
+        out_specs=vmem(),
         scratch_shapes=[
             pltpu.SMEM((LR, 8, NB), jnp.int32),
             pltpu.VMEM((LR, 1, B), jnp.int32),
             pltpu.VMEM((LR, LC, B, B), BF16),
             dma,
-            dma((LR,)),
             dma((LR,)),
             dma((LR,)),
         ],
@@ -457,7 +457,7 @@
     current = pl.pallas_call(
         schur_kernel,
         out_shape=like(LR, LC, B, B),
-        in_specs=[hbm()] + [anywhere()] * (NX + 2) + [vmem()] * 3 + [hbm()],
+        in_specs=[hbm()] + [anywhere()] * (NX + 2) + [vmem()] * 3,
         out_specs=hbm(),
         scratch_shapes=[
             pltpu.SMEM((8, NB), jnp.int32),
@@ -467,11 +467,10 @@
             dma((2 * NX,)),
             dma((LC,)),
         ],
-        input_output_aliases={NX + 6: 0},
         compiler_params=params(24),
         cost_estimate=cost(2 * LR * 12 * B**3, 90 * block),
         name="schur",
-    )(block_pattern, *held_rows, *other_rows, lower_mine, lower_neighbour, placed, current)
+    )(block_pattern, *held_rows, *other_rows, lower_mine, lower_neighbour, placed)
     return jnp.transpose(current, (0, 2, 1, 3)).reshape(matrix.shape)
 
 

time: 72.3 us -> 72 us (level)
  Pallas kernels: 13.3 us -> 11.4 us
  waiting for transfers between devices: 28.3 us -> 29.5 us
    pallas_call x1, Pallas kernels: 5.01 us -> 3.84 us  [local(): pl.pallas_call(permute_kernel, out_shape=pltpu.VMEM((LR, LC, B, B), BF16)...]
    ppermute x3, waiting for transfers between devices: 0.12 us -> 1.29 us  [local(): lax.ppermute(lower, 'pcol', [(0, 2 * d), (1, 2 * d + 1)])]
    pallas_call x1, Pallas kernels: 3.84 us -> 3.11 us  [local(): pl.pallas_call(schur_kernel, out_shape=like(LR, LC, B, B), in_specs=[hbm(...]
  transfers between devices with their start and end apart: 23 -> 23, of which waited for: 8 -> 8; matrix products, arithmetic and copies ran while one was open for 0% -> 0% of each run, Pallas kernels for 7% -> 6%
where the time goes in v1:
time: 72 us; the launch traced here: 71.3 us
  starting transfers between devices  29.9 us (42%)
  waiting for transfers between devices  29.5 us (41%)
  Pallas kernels  11.4 us (16%)
    ppermute x3, waiting for transfers between devices, local(): lax.ppermute(mine, 'prow', along_z(skip_z(skip)))  7.43 us
    ppermute x3, waiting for transfers between devices, gather_x(): return [own] + [lax.ppermute(own, 'prow', pairs) for pairs in shifted]  5.18 us
    ppermute x2, starting transfers between devices, spread_whole(): lax.ppermute(mine, axes, whole_pairs(p))  5.11 us
    ppermute x2, waiting for transfers between devices, local(): lax.ppermute(jnp.stack(held_rows[i:i + 2]), 'prow', along_z(ring_z(step)))  5.08 us
    ppermute x3, waiting for transfers between devices, scattered(): lax.ppermute(sent[d], 'prow', [(z, d * NZ + z) for z in range(2)])  4.73 us
    ppermute x3, starting transfers between devices, local(): lax.ppermute(lower, 'pcol', [(0, 2 * d), (1, 2 * d + 1)])  3.93 us
    ppermute x3, starting transfers between devices, local(): lax.ppermute(mine, 'prow', along_z(skip_z(skip)))  3.9 us
    ppermute x2, starting transfers between devices, local(): lax.ppermute(jnp.stack(held_rows[i:i + 2]), 'prow', along_z(ring_z(step)))  3.85 us
  transfers between devices with their start and end apart: 23, of which 8 were waited for; matrix products, arithmetic and copies ran while one was open for 0% of the time, Pallas kernels for 6%

profile of v1, /device:TPU:2, one launch (start us, length us, event | category | flops | bytes accessed | tf_op | source)
XLA Modules:
  0.0 71.3 jit_solution(11950207316412222023)
XLA Ops:
  0.0 2.0 %pack.1 = (bf16[4,6,64,256]{3,2,1,0:T(8,128)(2,1)S(1)}, bf16[256,256]{1,0:T(8,128)(2,1)S(1)}) custom-call(s32[96,96]{1,0:T(8,128)} %pattern_hbm.7, s32[3,1,256]{2,1,0:T(1,128)} %bitcast.28, bf16[3,12,256,256]{3,2,1,0:T(8,128)(2,1)} %bitcast.25), custom_call_target="tpu_custom_call" | custom-call | flops 234881024 | bytes 2490368 | tf_op jit(solution)/shard_map/pack/pallas_call | solution.py:388
  2.0 1.3 %collective-permute-start.13 = (bf16[256,256]{1,0:T(8,128)(2,1)S(1)}, bf16[256,256]{1,0:T(8,128)(2,1)S(1)}, u32[]{:S(2)}, u32[]{:S(2)}) collective-permute-start(bf16[256,256]{1,0:T(8,128)(2,1)S(1)} %get-tuple-element.13), channel_id=1, source_target_pairs={{0,64},{1,65},{9,73}} | collective-permute-start | bytes 393224 | tf_op jit(solution)/shard_map/ppermute | solution.py:337
  3.3 0.7 collective-permute-start.12
  4.0 0.7 collective-permute-start.11
  4.7 0.7 collective-permute-start.2
  5.4 0.7 collective-permute-start.1
  6.1 3.6 %collective-permute-done.13 = bf16[256,256]{1,0:T(8,128)(2,1)S(1)} collective-permute-done((bf16[256,256]{1,0:T(8,128)(2,1)S(1)}, bf16[256,256]{1,0:T(8,128)(2,1)S(1)}, u32[]{:S(2)}, u32[]{:S(2)}) %collective-permute-start.13) | collective-permute-done | bytes 131104 | tf_op jit(solution)/shard_map/ppermute | solution.py:337
  9.7 1.3 %collective-permute-start = (bf16[6,64,256]{2,1,0:T(8,128)(2,1)S(1)}, bf16[6,64,256]{2,1,0:T(8,128)(2,1)S(1)}, u32[]{:S(2)}, u32[]{:S(2)}) collective-permute-start(bf16[6,64,256]{2,1,0:T(8,128)(2,1)S(1)} %get-tuple-element.21), channel_id=1, source_target_pairs={{0,64},{8,72},{1,65},{9,73},{2,66},{10,74},{3,67},{11,75},{4,68},{... | collective-permute-start | bytes 589832 | tf_op jit(solution)/shard_map/ppermute | solution.py:314
  11.1 3.8 %collective-permute-start.15 = (bf16[256,256]{1,0:T(8,128)(2,1)S(1)}, bf16[256,256]{1,0:T(8,128)(2,1)S(1)}, u32[]{:S(2)}, u32[]{:S(2)}) collective-permute-start(bf16[256,256]{1,0:T(8,128)(2,1)S(1)} %select_select_fusion.refs_0_), channel_id=1, source_target_pairs={{0,40},{1,41},{64,104},{65,105},{128,168},{129,169},{192,232},{193... | collective-permute-start | bytes 393224 | tf_op jit(solution)/shard_map/ppermute | solution.py:338
  14.9 1.3 %collective-permute-start.14 = (bf16[256,256]{1,0:T(8,128)(2,1)S(1)}, bf16[256,256]{1,0:T(8,128)(2,1)S(1)}, u32[]{:S(2)}, u32[]{:S(2)}) collective-permute-start(bf16[256,256]{1,0:T(8,128)(2,1)S(1)} %select_select_fusion.refs_0_), channel_id=1, source_target_pairs={{0,24},{1,25},{64,88},{65,89},{128,152},{129,153},{192,216},{193,2... | collective-permute-start | bytes 393224 | tf_op jit(solution)/shard_map/ppermute | solution.py:338
  16.2 4.7 %collective-permute-done.refs_1_ = bf16[6,64,256]{2,1,0:T(8,128)(2,1)S(1)} collective-permute-done((bf16[6,64,256]{2,1,0:T(8,128)(2,1)S(1)}, bf16[6,64,256]{2,1,0:T(8,128)(2,1)S(1)}, u32[]{:S(2)}, u32[]{:S(2)}) %collective-permute-start) | collective-permute-done | bytes 196640 | tf_op jit(solution)/shard_map/ppermute | solution.py:314
  21.0 1.3 %collective-permute-start.5 = (bf16[6,64,256]{2,1,0:T(8,128)(2,1)S(1)}, bf16[6,64,256]{2,1,0:T(8,128)(2,1)S(1)}, u32[]{:S(2)}, u32[]{:S(2)}) collective-permute-start(bf16[6,64,256]{2,1,0:T(8,128)(2,1)S(1)} %select.8.refs_0_.refs_3_), channel_id=1, source_target_pairs={{0,32},{8,40},{64,96},{72,104},{128,160},{136,168},{192,224},{200,... | collective-permute-start | bytes 589832 | tf_op jit(solution)/shard_map/ppermute | solution.py:401
  22.3 1.3 %collective-permute-start.4 = (bf16[6,64,256]{2,1,0:T(8,128)(2,1)S(1)}, bf16[6,64,256]{2,1,0:T(8,128)(2,1)S(1)}, u32[]{:S(2)}, u32[]{:S(2)}) collective-permute-start(bf16[6,64,256]{2,1,0:T(8,128)(2,1)S(1)} %select.8.refs_0_.refs_3_), channel_id=1, source_target_pairs={{0,48},{8,56},{64,112},{72,120},{128,176},{136,184},{192,240},{200... | collective-permute-start | bytes 589832 | tf_op jit(solution)/shard_map/ppermute | solution.py:401
  23.6 1.3 %collective-permute-start.3 = (bf16[6,64,256]{2,1,0:T(8,128)(2,1)S(1)}, bf16[6,64,256]{2,1,0:T(8,128)(2,1)S(1)}, u32[]{:S(2)}, u32[]{:S(2)}) collective-permute-start(bf16[6,64,256]{2,1,0:T(8,128)(2,1)S(1)} %select.8.refs_0_.refs_3_), channel_id=1, source_target_pairs={{0,16},{8,24},{64,80},{72,88},{128,144},{136,152},{192,208},{200,2... | collective-permute-start | bytes 589832 | tf_op jit(solution)/shard_map/ppermute | solution.py:401
  24.9 1.3 %collective-permute-start.17 = (bf16[256,256]{1,0:T(8,128)(2,1)S(1)}, bf16[256,256]{1,0:T(8,128)(2,1)S(1)}, u32[]{:S(2)}, u32[]{:S(2)}) collective-permute-start(bf16[256,256]{1,0:T(8,128)(2,1)S(1)} %select.10.held_ref), channel_id=1, source_target_pairs={{0,56},{1,57},{24,16},{25,17},{64,120},{65,121},{88,80},{89,81},{1... | collective-permute-start | bytes 393224 | tf_op jit(solution)/shard_map/ppermute | solution.py:340
  26.3 2.5 %collective-permute-start.16 = (bf16[256,256]{1,0:T(8,128)(2,1)S(1)}, bf16[256,256]{1,0:T(8,128)(2,1)S(1)}, u32[]{:S(2)}, u32[]{:S(2)}) collective-permute-start(bf16[256,256]{1,0:T(8,128)(2,1)S(1)} %select.10.held_ref), channel_id=1, source_target_pairs={{0,8},{1,9},{24,32},{25,33},{40,48},{41,49},{64,72},{65,73},{88,96... | collective-permute-start | bytes 393224 | tf_op jit(solution)/shard_map/ppermute | solution.py:340
  28.8 7.4 %collective-permute-done.4.refs_2_ = bf16[6,64,256]{2,1,0:T(8,128)(2,1)S(1)} collective-permute-done((bf16[6,64,256]{2,1,0:T(8,128)(2,1)S(1)}, bf16[6,64,256]{2,1,0:T(8,128)(2,1)S(1)}, u32[]{:S(2)}, u32[]{:S(2)}) %collective-permute-start.4) | collective-permute-done | bytes 196640 | tf_op jit(solution)/shard_map/ppermute | solution.py:401
  36.2 2.1 %collective-permute-done.17.down_ref = bf16[256,256]{1,0:T(8,128)(2,1)S(1)} collective-permute-done((bf16[256,256]{1,0:T(8,128)(2,1)S(1)}, bf16[256,256]{1,0:T(8,128)(2,1)S(1)}, u32[]{:S(2)}, u32[]{:S(2)}) %collective-permute-start.17) | collective-permute-done | bytes 131104 | tf_op jit(solution)/shard_map/ppermute | solution.py:340
  38.3 2.3 %inverse.1 = (bf16[3,256,256]{2,1,0:T(8,128)(2,1)S(1)}, bf16[256,256]{1,0:T(8,128)(2,1)S(1)}, bf16[256,256]{1,0:T(8,128)(2,1)S(1)}, bf16[256,256]{1,0:T(8,128)(2,1)S(1)}, bf16[3,256,256]{2,1,0:T(8,128)(2,1)S(1)}) custom-call(bf16[256,256]{1,0:T(8,128)(2,1)S(1)} %select.10.held_ref, bf16[256,256]{1,0:T(8,128)(2,1)S(1)} %collective-permute-done.16.up_ref, ...), custom_call_target="tpu_custom_call" | custom-call | flops 603979776 | bytes 1572864 | tf_op jit(solution)/shard_map/inverse/pallas_call | solution.py:408
  40.7 1.4 %collective-permute-start.18 = (bf16[3,256,256]{2,1,0:T(8,128)(2,1)S(1)}, bf16[3,256,256]{2,1,0:T(8,128)(2,1)S(1)}, u32[]{:S(2)}, u32[]{:S(2)}) collective-permute-start(bf16[3,256,256]{2,1,0:T(8,128)(2,1)S(1)} %get-tuple-element.14.own_ref), channel_id=1, source_target_pairs={{0,1},{8,9},{16,17},{24,25},{32,33},{40,41},{48,49},{56,57},{64,65... | collective-permute-start | bytes 1179656 | tf_op jit(solution)/shard_map/ppermute | solution.py:425
  42.1 0.7 collective-permute-start.7
  42.8 1.8 %collective-permute-start.6 = (bf16[6,64,256]{2,1,0:T(8,128)(2,1)S(1)}, bf16[6,64,256]{2,1,0:T(8,128)(2,1)S(1)}, u32[]{:S(2)}, u32[]{:S(2)}) collective-permute-start(bf16[6,64,256]{2,1,0:T(8,128)(2,1)S(1)} %select.9.after.held0), channel_id=1, source_target_pairs={{0,64},{8,72},{16,80},{24,88},{32,96},{40,104},{48,112},{56,120},{... | collective-permute-start | bytes 589832 | tf_op jit(solution)/shard_map/ppermute | solution.py:346
  44.7 1.3 %collective-permute-start.21 = (bf16[3,256,256]{2,1,0:T(8,128)(2,1)S(1)}, bf16[3,256,256]{2,1,0:T(8,128)(2,1)S(1)}, u32[]{:S(2)}, u32[]{:S(2)}) collective-permute-start(bf16[3,256,256]{2,1,0:T(8,128)(2,1)S(1)} %second.1.after.refs_0_), channel_id=1, source_target_pairs={{0,4},{1,5},{8,12},{9,13},{16,20},{17,21},{24,28},{25,29},{32,36},... | collective-permute-start | bytes 1179656 | tf_op jit(solution)/shard_map/ppermute | solution.py:453
  46.0 1.3 %collective-permute-start.20 = (bf16[3,256,256]{2,1,0:T(8,128)(2,1)S(1)}, bf16[3,256,256]{2,1,0:T(8,128)(2,1)S(1)}, u32[]{:S(2)}, u32[]{:S(2)}) collective-permute-start(bf16[3,256,256]{2,1,0:T(8,128)(2,1)S(1)} %second.1.after.refs_0_), channel_id=1, source_target_pairs={{0,2},{1,3},{8,10},{9,11},{16,18},{17,19},{24,26},{25,27},{32,34},... | collective-permute-start | bytes 1179656 | tf_op jit(solution)/shard_map/ppermute | solution.py:453
  47.3 5.2 %collective-permute-done.8.held3 = bf16[6,64,256]{2,1,0:T(8,128)(2,1)S(1)} collective-permute-done((bf16[6,64,256]{2,1,0:T(8,128)(2,1)S(1)}, bf16[6,64,256]{2,1,0:T(8,128)(2,1)S(1)}, u32[]{:S(2)}, u32[]{:S(2)}) %collective-permute-start.8) | collective-permute-done | bytes 196640 | tf_op jit(solution)/shard_map/ppermute | solution.py:346
  52.5 1.3 %collective-permute-start.19 = (bf16[3,256,256]{2,1,0:T(8,128)(2,1)S(1)}, bf16[3,256,256]{2,1,0:T(8,128)(2,1)S(1)}, u32[]{:S(2)}, u32[]{:S(2)}) collective-permute-start(bf16[3,256,256]{2,1,0:T(8,128)(2,1)S(1)} %second.1.after.refs_0_), channel_id=1, source_target_pairs={{0,6},{1,7},{8,14},{9,15},{16,22},{17,23},{24,30},{25,31},{32,38},... | collective-permute-start | bytes 1179656 | tf_op jit(solution)/shard_map/ppermute | solution.py:453
  53.9 3.8 %collective-permute-start.10 = (bf16[2,6,64,256]{3,2,1,0:T(8,128)(2,1)S(1)}, bf16[2,6,64,256]{3,2,1,0:T(8,128)(2,1)S(1)}, u32[]{:S(2)}, u32[]{:S(2)}) collective-permute-start(bf16[2,6,64,256]{3,2,1,0:T(8,128)(2,1)S(1)} %pad_maximum_fusion.1), channel_id=1, source_target_pairs={{0,56},{8,0},{16,8},{24,16},{32,24},{40,32},{48,40},{56,48},{64,12... | collective-permute-start | bytes 1179656 | tf_op jit(solution)/shard_map/ppermute | solution.py:405
  57.8 3.8 %permute.1.refs_4_.placed = bf16[3,12,256,256]{3,2,1,0:T(8,128)(2,1)S(1)} custom-call(s32[96,96]{1,0:T(8,128)} %pattern_hbm.7, s32[3,1,256]{2,1,0:T(1,128)} %bitcast.30, bf16[3,12,256,256]{3,2,1,0:T(8,128)(2,1)} %bitcast.27, bf16[3,256,256]{2,1,0:T(8,128)(2,1)S(1)} %second.1.after.refs_0_), custom_call_target="tpu_custom_call" | custom-call | flops 1207959552 | bytes 9437184 | tf_op jit(solution)/shard_map/permute/pallas_call | solution.py:436
  61.6 1.3 %collective-permute-done.20.refs_2_ = bf16[3,256,256]{2,1,0:T(8,128)(2,1)S(1)} collective-permute-done((bf16[3,256,256]{2,1,0:T(8,128)(2,1)S(1)}, bf16[3,256,256]{2,1,0:T(8,128)(2,1)S(1)}, u32[]{:S(2)}, u32[]{:S(2)}) %collective-permute-start.20) | collective-permute-done | bytes 393248 | tf_op jit(solution)/shard_map/ppermute | solution.py:453
  63.1 1.5 %collective-permute-done.10.other23 = bf16[2,6,64,256]{3,2,1,0:T(8,128)(2,1)S(1)} collective-permute-done((bf16[2,6,64,256]{3,2,1,0:T(8,128)(2,1)S(1)}, bf16[2,6,64,256]{3,2,1,0:T(8,128)(2,1)S(1)}, u32[]{:S(2)}, u32[]{:S(2)}) %collective-permute-start.10) | collective-permute-done | bytes 393248 | tf_op jit(solution)/shard_map/ppermute | solution.py:405
  64.6 3.5 %collective-permute-done.9.other01 = bf16[2,6,64,256]{3,2,1,0:T(8,128)(2,1)S(1)} collective-permute-done((bf16[2,6,64,256]{3,2,1,0:T(8,128)(2,1)S(1)}, bf16[2,6,64,256]{3,2,1,0:T(8,128)(2,1)S(1)}, u32[]{:S(2)}, u32[]{:S(2)}) %collective-permute-start.9) | collective-permute-done | bytes 393248 | tf_op jit(solution)/shard_map/ppermute | solution.py:405
  68.2 3.1 %schur.1 = bf16[3,12,256,256]{3,2,1,0:T(8,128)(2,1)} custom-call(s32[96,96]{1,0:T(8,128)} %pattern_hbm.7, bf16[6,64,256]{2,1,0:T(8,128)(2,1)S(1)} %select.9.after.held0, bf16[6,64,256]{2,1,0:T(8,128)(2,1)S(1)} %collective-permute-done.6.held1, bf16[6,64,256]{2,1,0:T(8,128)(2,1)S(1)} %collective-permute-done.7.held2, ...), custom_call_target="tpu_custom_call" | custom-call | flops 1207959552 | bytes 11796480 | tf_op jit(solution)/shard_map/schur/pallas_call | solution.py:457
  (27 shorter events, 0.6 us)
Async XLA Ops:
  2.0 7.7 %collective-permute-start.13 = (bf16[256,256]{1,0:T(8,128)(2,1)S(1)}, bf16[256,256]{1,0:T(8,128)(2,1)S(1)}, u32[]{:S(2)}, u32[]{:S(2)}) collective-permute-start(bf16[256,256]{1,0:T(8,128)(2,1)S(1)} %get-tuple-element.13), channel_id=1, source_target_pairs={{0,64},{1,65},{9,73}} | collective-permute-start | bytes 393224 | tf_op jit(solution)/shard_map/ppermute | solution.py:337
  3.3 7.7 %collective-permute-start.12 = (bf16[256,256]{1,0:T(8,128)(2,1)S(1)}, bf16[256,256]{1,0:T(8,128)(2,1)S(1)}, u32[]{:S(2)}, u32[]{:S(2)}) collective-permute-start(bf16[256,256]{1,0:T(8,128)(2,1)S(1)} %get-tuple-element.13), channel_id=1, source_target_pairs={{0,128},{1,129},{9,137}} | collective-permute-start | bytes 393224 | tf_op jit(solution)/shard_map/ppermute | solution.py:337
  4.0 7.0 %collective-permute-start.11 = (bf16[256,256]{1,0:T(8,128)(2,1)S(1)}, bf16[256,256]{1,0:T(8,128)(2,1)S(1)}, u32[]{:S(2)}, u32[]{:S(2)}) collective-permute-start(bf16[256,256]{1,0:T(8,128)(2,1)S(1)} %get-tuple-element.13), channel_id=1, source_target_pairs={{0,192},{1,193},{9,201}} | collective-permute-start | bytes 393224 | tf_op jit(solution)/shard_map/ppermute | solution.py:337
  4.7 11.5 %collective-permute-start.2 = (bf16[6,64,256]{2,1,0:T(8,128)(2,1)S(1)}, bf16[6,64,256]{2,1,0:T(8,128)(2,1)S(1)}, u32[]{:S(2)}, u32[]{:S(2)}) collective-permute-start(bf16[6,64,256]{2,1,0:T(8,128)(2,1)S(1)} %get-tuple-element.19), channel_id=1, source_target_pairs={{0,192},{8,200},{1,193},{9,201},{2,194},{10,202},{3,195},{11,203},... | collective-permute-start | bytes 589832 | tf_op jit(solution)/shard_map/ppermute | solution.py:314
  5.4 10.8 %collective-permute-start.1 = (bf16[6,64,256]{2,1,0:T(8,128)(2,1)S(1)}, bf16[6,64,256]{2,1,0:T(8,128)(2,1)S(1)}, u32[]{:S(2)}, u32[]{:S(2)}) collective-permute-start(bf16[6,64,256]{2,1,0:T(8,128)(2,1)S(1)} %get-tuple-element.20), channel_id=1, source_target_pairs={{0,128},{8,136},{1,129},{9,137},{2,130},{10,138},{3,131},{11,139},... | collective-permute-start | bytes 589832 | tf_op jit(solution)/shard_map/ppermute | solution.py:314
  9.7 11.2 %collective-permute-start = (bf16[6,64,256]{2,1,0:T(8,128)(2,1)S(1)}, bf16[6,64,256]{2,1,0:T(8,128)(2,1)S(1)}, u32[]{:S(2)}, u32[]{:S(2)}) collective-permute-start(bf16[6,64,256]{2,1,0:T(8,128)(2,1)S(1)} %get-tuple-element.21), channel_id=1, source_target_pairs={{0,64},{8,72},{1,65},{9,73},{2,66},{10,74},{3,67},{11,75},{4,68},{... | collective-permute-start | bytes 589832 | tf_op jit(solution)/shard_map/ppermute | solution.py:314
  11.1 13.8 %collective-permute-start.15 = (bf16[256,256]{1,0:T(8,128)(2,1)S(1)}, bf16[256,256]{1,0:T(8,128)(2,1)S(1)}, u32[]{:S(2)}, u32[]{:S(2)}) collective-permute-start(bf16[256,256]{1,0:T(8,128)(2,1)S(1)} %select_select_fusion.refs_0_), channel_id=1, source_target_pairs={{0,40},{1,41},{64,104},{65,105},{128,168},{129,169},{192,232},{193... | collective-permute-start | bytes 393224 | tf_op jit(solution)/shard_map/ppermute | solution.py:338
  14.9 10.0 %collective-permute-start.14 = (bf16[256,256]{1,0:T(8,128)(2,1)S(1)}, bf16[256,256]{1,0:T(8,128)(2,1)S(1)}, u32[]{:S(2)}, u32[]{:S(2)}) collective-permute-start(bf16[256,256]{1,0:T(8,128)(2,1)S(1)} %select_select_fusion.refs_0_), channel_id=1, source_target_pairs={{0,24},{1,25},{64,88},{65,89},{128,152},{129,153},{192,216},{193,2... | collective-permute-start | bytes 393224 | tf_op jit(solution)/shard_map/ppermute | solution.py:338
  21.0 7.8 %collective-permute-start.5 = (bf16[6,64,256]{2,1,0:T(8,128)(2,1)S(1)}, bf16[6,64,256]{2,1,0:T(8,128)(2,1)S(1)}, u32[]{:S(2)}, u32[]{:S(2)}) collective-permute-start(bf16[6,64,256]{2,1,0:T(8,128)(2,1)S(1)} %select.8.refs_0_.refs_3_), channel_id=1, source_target_pairs={{0,32},{8,40},{64,96},{72,104},{128,160},{136,168},{192,224},{200,... | collective-permute-start | bytes 589832 | tf_op jit(solution)/shard_map/ppermute | solution.py:401
  22.3 13.9 %collective-permute-start.4 = (bf16[6,64,256]{2,1,0:T(8,128)(2,1)S(1)}, bf16[6,64,256]{2,1,0:T(8,128)(2,1)S(1)}, u32[]{:S(2)}, u32[]{:S(2)}) collective-permute-start(bf16[6,64,256]{2,1,0:T(8,128)(2,1)S(1)} %select.8.refs_0_.refs_3_), channel_id=1, source_target_pairs={{0,48},{8,56},{64,112},{72,120},{128,176},{136,184},{192,240},{200... | collective-permute-start | bytes 589832 | tf_op jit(solution)/shard_map/ppermute | solution.py:401
  23.6 12.6 %collective-permute-start.3 = (bf16[6,64,256]{2,1,0:T(8,128)(2,1)S(1)}, bf16[6,64,256]{2,1,0:T(8,128)(2,1)S(1)}, u32[]{:S(2)}, u32[]{:S(2)}) collective-permute-start(bf16[6,64,256]{2,1,0:T(8,128)(2,1)S(1)} %select.8.refs_0_.refs_3_), channel_id=1, source_target_pairs={{0,16},{8,24},{64,80},{72,88},{128,144},{136,152},{192,208},{200,2... | collective-permute-start | bytes 589832 | tf_op jit(solution)/shard_map/ppermute | solution.py:401
  24.9 13.4 %collective-permute-start.17 = (bf16[256,256]{1,0:T(8,128)(2,1)S(1)}, bf16[256,256]{1,0:T(8,128)(2,1)S(1)}, u32[]{:S(2)}, u32[]{:S(2)}) collective-permute-start(bf16[256,256]{1,0:T(8,128)(2,1)S(1)} %select.10.held_ref), channel_id=1, source_target_pairs={{0,56},{1,57},{24,16},{25,17},{64,120},{65,121},{88,80},{89,81},{1... | collective-permute-start | bytes 393224 | tf_op jit(solution)/shard_map/ppermute | solution.py:340
  26.3 12.1 %collective-permute-start.16 = (bf16[256,256]{1,0:T(8,128)(2,1)S(1)}, bf16[256,256]{1,0:T(8,128)(2,1)S(1)}, u32[]{:S(2)}, u32[]{:S(2)}) collective-permute-start(bf16[256,256]{1,0:T(8,128)(2,1)S(1)} %select.10.held_ref), channel_id=1, source_target_pairs={{0,8},{1,9},{24,32},{25,33},{40,48},{41,49},{64,72},{65,73},{88,96... | collective-permute-start | bytes 393224 | tf_op jit(solution)/shard_map/ppermute | solution.py:340
  40.7 4.0 %collective-permute-start.18 = (bf16[3,256,256]{2,1,0:T(8,128)(2,1)S(1)}, bf16[3,256,256]{2,1,0:T(8,128)(2,1)S(1)}, u32[]{:S(2)}, u32[]{:S(2)}) collective-permute-start(bf16[3,256,256]{2,1,0:T(8,128)(2,1)S(1)} %get-tuple-element.14.own_ref), channel_id=1, source_target_pairs={{0,1},{8,9},{16,17},{24,25},{32,33},{40,41},{48,49},{56,57},{64,65... | collective-permute-start | bytes 1179656 | tf_op jit(solution)/shard_map/ppermute | solution.py:425
  42.0 10.5 %collective-permute-start.8 = (bf16[6,64,256]{2,1,0:T(8,128)(2,1)S(1)}, bf16[6,64,256]{2,1,0:T(8,128)(2,1)S(1)}, u32[]{:S(2)}, u32[]{:S(2)}) collective-permute-start(bf16[6,64,256]{2,1,0:T(8,128)(2,1)S(1)} %select.9.after.held0), channel_id=1, source_target_pairs={{0,192},{8,200},{16,208},{24,216},{32,224},{40,232},{48,240},{56,2... | collective-permute-start | bytes 589832 | tf_op jit(solution)/shard_map/ppermute | solution.py:346
  42.1 11.7 %collective-permute-start.7 = (bf16[6,64,256]{2,1,0:T(8,128)(2,1)S(1)}, bf16[6,64,256]{2,1,0:T(8,128)(2,1)S(1)}, u32[]{:S(2)}, u32[]{:S(2)}) collective-permute-start(bf16[6,64,256]{2,1,0:T(8,128)(2,1)S(1)} %select.9.after.held0), channel_id=1, source_target_pairs={{0,128},{8,136},{16,144},{24,152},{32,160},{40,168},{48,176},{56,1... | collective-permute-start | bytes 589832 | tf_op jit(solution)/shard_map/ppermute | solution.py:346
  42.8 14.8 %collective-permute-start.6 = (bf16[6,64,256]{2,1,0:T(8,128)(2,1)S(1)}, bf16[6,64,256]{2,1,0:T(8,128)(2,1)S(1)}, u32[]{:S(2)}, u32[]{:S(2)}) collective-permute-start(bf16[6,64,256]{2,1,0:T(8,128)(2,1)S(1)} %select.9.after.held0), channel_id=1, source_target_pairs={{0,64},{8,72},{16,80},{24,88},{32,96},{40,104},{48,112},{56,120},{... | collective-permute-start | bytes 589832 | tf_op jit(solution)/shard_map/ppermute | solution.py:346
  44.7 16.9 %collective-permute-start.21 = (bf16[3,256,256]{2,1,0:T(8,128)(2,1)S(1)}, bf16[3,256,256]{2,1,0:T(8,128)(2,1)S(1)}, u32[]{:S(2)}, u32[]{:S(2)}) collective-permute-start(bf16[3,256,256]{2,1,0:T(8,128)(2,1)S(1)} %second.1.after.refs_0_), channel_id=1, source_target_pairs={{0,4},{1,5},{8,12},{9,13},{16,20},{17,21},{24,28},{25,29},{32,36},... | collective-permute-start | bytes 1179656 | tf_op jit(solution)/shard_map/ppermute | solution.py:453
  46.0 16.9 %collective-permute-start.20 = (bf16[3,256,256]{2,1,0:T(8,128)(2,1)S(1)}, bf16[3,256,256]{2,1,0:T(8,128)(2,1)S(1)}, u32[]{:S(2)}, u32[]{:S(2)}) collective-permute-start(bf16[3,256,256]{2,1,0:T(8,128)(2,1)S(1)} %second.1.after.refs_0_), channel_id=1, source_target_pairs={{0,2},{1,3},{8,10},{9,11},{16,18},{17,19},{24,26},{25,27},{32,34},... | collective-permute-start | bytes 1179656 | tf_op jit(solution)/shard_map/ppermute | solution.py:453
  52.5 10.4 %collective-permute-start.19 = (bf16[3,256,256]{2,1,0:T(8,128)(2,1)S(1)}, bf16[3,256,256]{2,1,0:T(8,128)(2,1)S(1)}, u32[]{:S(2)}, u32[]{:S(2)}) collective-permute-start(bf16[3,256,256]{2,1,0:T(8,128)(2,1)S(1)} %second.1.after.refs_0_), channel_id=1, source_target_pairs={{0,6},{1,7},{8,14},{9,15},{16,22},{17,23},{24,30},{25,31},{32,38},... | collective-permute-start | bytes 1179656 | tf_op jit(solution)/shard_map/ppermute | solution.py:453
  53.9 10.7 %collective-permute-start.10 = (bf16[2,6,64,256]{3,2,1,0:T(8,128)(2,1)S(1)}, bf16[2,6,64,256]{3,2,1,0:T(8,128)(2,1)S(1)}, u32[]{:S(2)}, u32[]{:S(2)}) collective-permute-start(bf16[2,6,64,256]{3,2,1,0:T(8,128)(2,1)S(1)} %pad_maximum_fusion.1), channel_id=1, source_target_pairs={{0,56},{8,0},{16,8},{24,16},{32,24},{40,32},{48,40},{56,48},{64,12... | collective-permute-start | bytes 1179656 | tf_op jit(solution)/shard_map/ppermute | solution.py:405
  57.7 10.5 %collective-permute-start.9 = (bf16[2,6,64,256]{3,2,1,0:T(8,128)(2,1)S(1)}, bf16[2,6,64,256]{3,2,1,0:T(8,128)(2,1)S(1)}, u32[]{:S(2)}, u32[]{:S(2)}) collective-permute-start(bf16[2,6,64,256]{3,2,1,0:T(8,128)(2,1)S(1)} %pad_maximum_fusion), channel_id=1, source_target_pairs={{0,8},{8,16},{16,24},{24,32},{32,40},{40,48},{48,56},{56,0},{64,72... | collective-permute-start | bytes 1179656 | tf_op jit(solution)/shard_map/ppermute | solution.py:405
  63.0 5.2 %collective-permute-start.22 = (bf16[3,256,256]{2,1,0:T(8,128)(2,1)S(1)}, bf16[3,256,256]{2,1,0:T(8,128)(2,1)S(1)}, u32[]{:S(2)}, u32[]{:S(2)}) collective-permute-start(bf16[3,256,256]{2,1,0:T(8,128)(2,1)S(1)} %select.11.mine_ref), channel_id=1, source_target_pairs={{0,1},{1,0},{2,3},{3,2},{4,5},{5,4},{6,7},{7,6},{8,9},{9,8},{10,11... | collective-permute-start | bytes 1179656 | tf_op jit(solution)/shard_map/ppermute | solution.py:455
